TPU v7x, 32 devices: a whole 2x2x4 slice. The times are simulated.
32 devices in a mesh: node: 4 (over y, x), grid: 8 (over z, core).
Axes of the slice: x: 2, y: 2, z: 4, core: 2. Of those that a mesh axis runs over, the one named last changes fastest.
Arguments:
- probes: float32 [1, 48, 192, 256], P(None, 'grid'), may hold values from -6 to 6
- potential: float32 [48, 192, 256], P('grid'), may hold values from -2 to 1
- warm_start: bfloat16 [4, 1, 2, 48, 192, 256], P('node', None, None, 'grid'), may hold values from -0.29882812 to 0.29882812
- shift_points: float32 [4, 2], P('node'), may hold values from -4 to 9, as said below
- quad_weights: float32 [4, 2], P('node'), may hold values from -0.3 to 0.3
Outputs:
- moments: float32 [2, 1, 2, 48, 192, 256], P(None, None, None, 'grid', 'node')
- trace_estimate: float32 [2], replicated
Inputs may be any that keep to these rules, and one draw needn't show every extreme that they name: `shift_points`: column 0 holds real parts in -1 to 9; column 1 holds imaginary parts whose magnitude lies in 1 to 4.
All inputs are finite; a program needn't handle non-finite values.
Results may differ from a plain program's by a relative error of at most 0.0003.
Values may be sent and summed in bfloat16 or wider, within the bound.
A program may use at most 192 MiB of HBM per device.

v0:
```python
import jax
import jax.numpy as jnp
from jax import lax
from jax.sharding import PartitionSpec as P

PROBES = 1
ITERS = 2
MOMENTS = 2
near_weight = 4.0 / 3.0
far_weight = -1.0 / 12.0
self_weight = -7.5


def with_halo(cells, sides, width):
    for axis, dim in sides:
        count = lax.axis_size(axis)
        head = lax.slice_in_dim(cells, 0, width, axis=dim)
        tail = lax.slice_in_dim(cells, cells.shape[dim] - width, cells.shape[dim], axis=dim)
        cells = jnp.concatenate(
            [
                lax.ppermute(tail, axis, [(i, (i + 1) % count) for i in range(count)]),
                cells,
                lax.ppermute(head, axis, [((i + 1) % count, i) for i in range(count)]),
            ],
            axis=dim,
        )
    return cells


def hamiltonian_apply(padded, potential, shift_real, shift_imag):
    middle = padded[:, :, :, 2:-2]
    near_sum = (
        padded[:, :, :, 1:-3]
        + padded[:, :, :, 3:-1]
        + (jnp.roll(middle, 1, 4) + jnp.roll(middle, -1, 4))
        + (jnp.roll(middle, 1, 5) + jnp.roll(middle, -1, 5))
    )
    far_sum = (
        padded[:, :, :, :-4]
        + padded[:, :, :, 4:]
        + (jnp.roll(middle, 2, 4) + jnp.roll(middle, -2, 4))
        + (jnp.roll(middle, 2, 5) + jnp.roll(middle, -2, 5))
    )
    laplacian = near_weight * near_sum + far_weight * far_sum + self_weight * middle
    real_shift = shift_real[:, None, None, None, None]
    imag_shift = shift_imag[:, None, None, None, None]
    real_part = middle[:, :, 0]
    imag_part = middle[:, :, 1]
    result_real = (
        real_shift * real_part
        - imag_shift * imag_part
        + 0.5 * laplacian[:, :, 0]
        - potential * real_part
    )
    result_imag = (
        real_shift * imag_part
        + imag_shift * real_part
        + 0.5 * laplacian[:, :, 1]
        - potential * imag_part
    )
    return jnp.stack([result_real, result_imag], axis=2)


def bilinear(first_vec, second_vec):
    real_sum = jnp.sum(
        first_vec[:, :, 0] * second_vec[:, :, 0] - first_vec[:, :, 1] * second_vec[:, :, 1],
        axis=(2, 3, 4),
    )
    imag_sum = jnp.sum(
        first_vec[:, :, 0] * second_vec[:, :, 1] + first_vec[:, :, 1] * second_vec[:, :, 0],
        axis=(2, 3, 4),
    )
    return jnp.stack([real_sum, imag_sum], axis=-1)


def complex_times(factor_one, factor_two):
    return jnp.stack(
        [
            factor_one[..., 0] * factor_two[..., 0] - factor_one[..., 1] * factor_two[..., 1],
            factor_one[..., 0] * factor_two[..., 1] + factor_one[..., 1] * factor_two[..., 0],
        ],
        axis=-1,
    )


def complex_divide(factor_one, factor_two):
    magnitude = factor_two[..., 0] * factor_two[..., 0] + factor_two[..., 1] * factor_two[..., 1]
    return jnp.stack(
        [
            (factor_one[..., 0] * factor_two[..., 0] + factor_one[..., 1] * factor_two[..., 1])
            / magnitude,
            (factor_one[..., 1] * factor_two[..., 0] - factor_one[..., 0] * factor_two[..., 1])
            / magnitude,
        ],
        axis=-1,
    )


def scale_field(scalars, vector):
    real_scalar = scalars[..., 0][:, :, None, None, None]
    imag_scalar = scalars[..., 1][:, :, None, None, None]
    return jnp.stack(
        [
            real_scalar * vector[:, :, 0] - imag_scalar * vector[:, :, 1],
            real_scalar * vector[:, :, 1] + imag_scalar * vector[:, :, 0],
        ],
        axis=2,
    )


def trim_planes(vector, extent_now, extent_out, along_dim):
    excess = extent_now - extent_out
    if excess == 0:
        return vector
    return lax.slice_in_dim(vector, excess, vector.shape[along_dim] - excess, axis=along_dim)


def center(vector, extent):
    return trim_planes(vector, extent, 0, 3)


def residual_norms(vector):
    return lax.psum(bilinear(vector, vector), "grid")


def per_device(probes, potential, warm_start, shift_points, quad_weights):
    shift_real = shift_points[:, 0]
    shift_imag = shift_points[:, 1]
    start_width = 2
    start_wide = with_halo(warm_start, (("grid", 3),), start_width).astype(jnp.float32)
    start_extent = start_width - 2
    solution = warm_start.astype(jnp.float32)
    potential_extent = 0
    source = jnp.stack([probes, jnp.zeros_like(probes)], axis=1)[None]
    residual = source - hamiltonian_apply(
        start_wide,
        trim_planes(potential, potential_extent, start_extent, 0),
        shift_real,
        shift_imag,
    )
    direction = residual
    extent = start_extent
    residual_extent = start_extent
    norm_now = residual_norms(center(residual, start_extent))
    for iteration in range(ITERS):
        padded = with_halo(direction, (("grid", 3),), 2)
        margin = 2
        extent_out = margin - 2
        applied = hamiltonian_apply(
            padded, trim_planes(potential, potential_extent, extent_out, 0), shift_real, shift_imag
        )
        applied, direction, extent = (
            applied,
            trim_planes(padded, margin, extent_out, 3),
            extent_out,
        )
        if iteration == 0:
            residual = direction
            residual_extent = extent
        center_part = center(direction, extent)
        curvature = lax.psum(bilinear(center_part, center(applied, extent)), "grid")
        step_length = complex_divide(norm_now, curvature)
        solution = solution + scale_field(step_length, center_part)
        residual = trim_planes(residual, residual_extent, extent, 3) - scale_field(
            step_length, applied
        )
        residual_extent = extent
        if iteration + 1 < ITERS:
            norm_next = residual_norms(center(residual, extent))
            direction = residual + scale_field(complex_divide(norm_next, norm_now), direction)
            norm_now = norm_next
    scaled_shift = jnp.stack([(shift_real - 4.0) / 5.0, shift_imag / 5.0], axis=-1)
    weight_power = quad_weights
    powers = []
    for degree in range(MOMENTS):
        powers.append(weight_power)
        weight_power = complex_times(weight_power, scaled_shift)
    coefficients = jnp.stack(powers)
    coef_real = coefficients[..., 0]
    coef_imag = coefficients[..., 1]
    highest = lax.Precision.HIGHEST
    sol_real = solution[:, :, 0]
    sol_imag = solution[:, :, 1]
    term_real = jnp.einsum("ks,spzxy->kpzxy", coef_real, sol_real, precision=highest) - jnp.einsum(
        "ks,spzxy->kpzxy", coef_imag, sol_imag, precision=highest
    )
    term_imag = jnp.einsum("ks,spzxy->kpzxy", coef_real, sol_imag, precision=highest) + jnp.einsum(
        "ks,spzxy->kpzxy", coef_imag, sol_real, precision=highest
    )
    moment_terms = jnp.stack([term_real, term_imag], axis=2)
    moments = lax.psum_scatter(moment_terms, "node", scatter_dimension=4, tiled=True)
    inner_sums = jnp.einsum("pzxy,spczxy->sc", probes, solution, precision=highest) / PROBES
    local_trace = jnp.sum(complex_times(quad_weights, inner_sums), axis=0)
    trace_estimate = lax.psum(local_trace, ("node", "grid"))
    return (moments, trace_estimate)


def solution(mesh):
    return jax.shard_map(
        per_device,
        mesh=mesh,
        in_specs=(
            P(None, "grid", None, None),
            P("grid", None, None),
            P("node", None, None, "grid", None, None),
            P("node", None),
            P("node", None),
        ),
        out_specs=(P(None, None, None, "grid", "node", None), P()),
        check_vma=False,
    )
```

profile of v0, /device:TPU:12, one launch (start us, length us, event | category | flops | bytes accessed | tf_op | source)
XLA Modules:
  0.0 308.9 jit_solution(7874606106377025501)
XLA Ops:
  15.6 2.4 collective-permute-done
  18.8 2.2 fusion.79
  22.4 2.6 fusion.78
  25.0 2.9 fusion.76
  29.8 8.3 %fusion.24 = f32[1,1,2,6,192,256]{5,4,3,2,1,0:T(8,128)} fusion(f32[1,1,2,10,192,256]{5,4,3,2,1,0:T(8,128)S(1)} %maximum_convert_fusion, f32[1,1,2,6,191,256]{5,4,3,2,1,0:T(8,128)S(1)} %get-tuple-element.31, f32[1,1,2,6,1,256]{5,4,3,2,1,0:T(1,128)S(1)} %get-tuple-element.83, f32[1,1,2,6,1,256]{5,4,3,2,1,0:T(1,128)S(1)} %get-tuple-element.82, ...), kind=kLoop, calls=%fused_computation.38 | loop fusion | flops 13565952 | bytes 33030144 | tf_op jit(solution)/shard_map/add | solution.py:44
  38.1 3.6 %fusion.54 = (f32[1,1,1,6,192,256]{5,4,3,2,1,0:T(8,128)S(1)}, f32[1,1,1,6,192,256]{5,4,3,2,1,0:T(8,128)S(1)}) fusion(f32[1,1,2,6,192,256]{5,4,3,2,1,0:T(8,128)} %fusion.24, f32[6,192,256]{2,1,0:T(8,128)S(1)} %copy-done.7, f32[1,1,2,10,192,256]{5,4,3,2,1,0:T(8,128)S(1)} %maximum_convert_fusion, f32[]{:T(128)} %bitcast.6, f32[]{:T(128)} %bitcast.4), kind=kLoop, calls=%fused_computation.97 | loop fusion | flops 4128768 | bytes 8257544 | tf_op jit(solution)/shard_map/stack | solution.py:61
  45.0 3.0 fusion.95
  52.8 1.9 pad_maximum_fusion.6
  54.7 2.6 fusion.93
  57.3 2.9 fusion.91
  60.2 3.1 %collective-permute-done.3 = f32[1,1,2,2,192,256]{5,4,3,2,1,0:T(8,128)S(1)} collective-permute-done((f32[1,1,2,2,192,256]{5,4,3,2,1,0:T(8,128)S(1)}, f32[1,1,2,2,192,256]{5,4,3,2,1,0:T(8,128)S(1)}, u32[]{:S(2)}, u32[]{:S(2)}) %collective-permute-start.3) | collective-permute-done | bytes 786464 | tf_op jit(solution)/shard_map/ppermute | solution.py:23
  63.3 10.7 %collective-permute-done.2 = f32[1,1,2,2,192,256]{5,4,3,2,1,0:T(8,128)S(1)} collective-permute-done((f32[1,1,2,2,192,256]{5,4,3,2,1,0:T(8,128)S(1)}, f32[1,1,2,2,192,256]{5,4,3,2,1,0:T(8,128)S(1)}, u32[]{:S(2)}, u32[]{:S(2)}) %collective-permute-start.2) | collective-permute-done | bytes 786464 | tf_op jit(solution)/shard_map/ppermute | solution.py:21
  74.9 9.1 %fusion.14 = f32[1,1,2,6,192,256]{5,4,3,2,1,0:T(8,128)S(1)} fusion(f32[1,1,2,6,192,256]{5,4,3,2,1,0:T(8,128)S(1)} %maximum_subtract_fusion, f32[1,1,2,2,192,256]{5,4,3,2,1,0:T(8,128)} %copy-done.23, f32[1,1,2,2,192,256]{5,4,3,2,1,0:T(8,128)} %copy-done.24, f32[1,1,2,6,191,256]{5,4,3,2,1,0:T(8,128)} %get-tuple-element.75, ...), kind=kLoop, calls=%fused_computation.23 | loop fusion | flops 15925248 | bytes 25165824 | tf_op jit(solution)/shard_map/add | solution.py:44
  84.0 4.3 %fusion.64 = (f32[]{:T(128)}, f32[]{:T(128)}, f32[6,192,256]{2,1,0:T(8,128)}, f32[6,192,256]{2,1,0:T(8,128)}) fusion(f32[1,1,2,6,192,256]{5,4,3,2,1,0:T(8,128)S(1)} %maximum_subtract_fusion, f32[6,192,256]{2,1,0:T(8,128)S(1)} %copy-done.7, f32[1,1,2,6,192,256]{5,4,3,2,1,0:T(8,128)S(1)} %fusion.14, f32[]{:T(128)} %bitcast.6, f32[]{:T(128)} %bitcast.4), kind=kLoop, calls=%fused_computation.124 | loop fusion | flops 6488062 | bytes 8257552 | tf_op jit(solution)/shard_map/reduce_sum | solution.py:65
  90.2 14.2 %all-reduce.1 = (f32[1,1,2]{2,1,0:T(1,128)S(1)}, f32[1,1,2]{2,1,0:T(1,128)S(1)}) all-reduce(f32[1,1,2]{2,1,0:T(1,128)S(1)} %copy-done.28, f32[1,1,2]{2,1,0:T(1,128)} %pad_maximum_fusion.7), channel_id=1, replica_groups=mesh['node'=4,'grid'=8] {'grid'}, use_global_device_ids=true, to_apply=%region_2.3 | all-reduce | flops 4 | bytes 32 | tf_op jit(solution)/shard_map/psum | solution.py:123
  114.1 2.1 subtract_bitcast_fusion.1
  121.4 13.6 %psum.37 = f32[1,1,2]{2,1,0:T(1,128)S(1)} all-reduce(f32[1,1,2]{2,1,0:T(1,128)S(1)} %pad_maximum_fusion.8), channel_id=1, replica_groups=mesh['node'=4,'grid'=8] {'grid'}, use_global_device_ids=true, to_apply=%region_8.9 | all-reduce | flops 2 | bytes 16 | tf_op jit(solution)/shard_map/psum | solution.py:123
  141.0 1.9 multiply_subtract_fusion.1
  145.6 3.0 fusion.86
  150.0 1.8 fusion.83
  151.9 3.6 %collective-permute-start.5 = (f32[1,1,2,2,192,256]{5,4,3,2,1,0:T(8,128)S(1)}, f32[1,1,2,2,192,256]{5,4,3,2,1,0:T(8,128)S(1)}, u32[]{:S(2)}, u32[]{:S(2)}) collective-permute-start(f32[1,1,2,2,192,256]{5,4,3,2,1,0:T(8,128)S(1)} %get-tuple-element.55), channel_id=1, source_target_pairs={{1,0},{2,1},{3,2},{4,3},{5,4},{6,5},{7,6},{0,7},{9,8},{10,9},{11,1... | collective-permute-start | bytes 2359304 | tf_op jit(solution)/shard_map/ppermute | solution.py:23
  155.4 2.6 fusion.84
  158.1 2.9 fusion.82
  161.0 12.4 %collective-permute-done.5 = f32[1,1,2,2,192,256]{5,4,3,2,1,0:T(8,128)S(1)} collective-permute-done((f32[1,1,2,2,192,256]{5,4,3,2,1,0:T(8,128)S(1)}, f32[1,1,2,2,192,256]{5,4,3,2,1,0:T(8,128)S(1)}, u32[]{:S(2)}, u32[]{:S(2)}) %collective-permute-start.5) | collective-permute-done | bytes 786464 | tf_op jit(solution)/shard_map/ppermute | solution.py:23
  175.3 9.9 %fusion.6 = f32[1,1,2,6,192,256]{5,4,3,2,1,0:T(8,128)} fusion(f32[1,1,2,6,192,256]{5,4,3,2,1,0:T(8,128)S(1)} %maximum_add_fusion.9, f32[1,1,2,2,192,256]{5,4,3,2,1,0:T(8,128)} %copy-done.25, f32[1,1,2,2,192,256]{5,4,3,2,1,0:T(8,128)} %copy-done.26, f32[1,1,2,6,191,256]{5,4,3,2,1,0:T(8,128)S(1)} %get-tuple-element.51, ...), kind=kLoop, calls=%fused_computation.15 | loop fusion | flops 15925248 | bytes 25165824 | tf_op jit(solution)/shard_map/add | solution.py:44
  185.2 3.5 %fusion.40 = (f32[6,192,256]{2,1,0:T(8,128)S(1)}, f32[6,192,256]{2,1,0:T(8,128)S(1)}) fusion(f32[1,1,2,6,192,256]{5,4,3,2,1,0:T(8,128)} %fusion.6, f32[6,192,256]{2,1,0:T(8,128)S(1)} %copy-done.8, f32[1,1,2,6,192,256]{5,4,3,2,1,0:T(8,128)S(1)} %maximum_add_fusion.9, f32[]{:T(128)} %bitcast.6, f32[]{:T(128)} %bitcast.4), kind=kLoop, calls=%fused_computation.79 | loop fusion | flops 4128768 | bytes 8257544 | tf_op jit(solution)/shard_map/sub | solution.py:50
  189.9 2.0 pad_maximum_fusion.9
  192.1 12.2 %psum.38 = f32[1,1,2]{2,1,0:T(1,128)S(1)} all-reduce(f32[1,1,2]{2,1,0:T(1,128)} %pad_maximum_fusion.9), channel_id=1, replica_groups=mesh['node'=4,'grid'=8] {'grid'}, use_global_device_ids=true, to_apply=%region_11.12 | all-reduce | flops 2 | bytes 16 | tf_op jit(solution)/shard_map/psum | solution.py:161
  216.5 2.6 pad_maximum_fusion
  220.8 2.1 fusion.108
  222.9 29.6 %fusion.68 = f32[1,2]{1,0:T(1,128)S(1)} fusion(f32[6,192,256,1]{2,1,0,3:T(8,128)S(1)} %bitcast.197, f32[2,6,192,256]{3,2,1,0:T(8,128)S(1)} %fusion.108), kind=kOutput, calls=%fused_computation.145 | convolution fusion | flops 7077888 | bytes 3538952 | tf_op jit(solution)/shard_map/pzxy,spczxy->sc/dot_general | solution.py:192
  258.1 44.0 %psum.39 = f32[2]{0:T(128)} all-reduce(f32[2]{0:T(128)S(1)} %maximum_bitcast_fusion.1), channel_id=1, replica_groups=mesh['node'=4,'grid'=8] {'node','grid'}, use_global_device_ids=true, to_apply=%region_13.14 | all-reduce | flops 2 | bytes 16 | tf_op jit(solution)/shard_map/psum | solution.py:194
  (107 shorter events, 38.7 us)
Async XLA Ops:
  7.2 10.8 %copy-start = (bf16[1,1,2,6,192,256]{5,4,3,2,1,0:T(8,128)(2,1)S(1)}, bf16[1,1,2,6,192,256]{5,4,3,2,1,0:T(8,128)(2,1)}, u32[]{:S(2)}) copy-start(bf16[1,1,2,6,192,256]{5,4,3,2,1,0:T(8,128)(2,1)} %param.7) | copy-start | bytes 3538948
  7.2 294.9 %reduce-scatter.2.cloned.1.call-start = ((), (), s32[]{:S(2)}) async-start(), calls=%async_computation.1 | async-start | bytes 5898240 | tf_op jit(solution)/shard_map/reduce_scatter | solution.py:191
  8.5 7.1 %collective-permute-start.1 = (bf16[1,1,2,2,192,256]{5,4,3,2,1,0:T(8,128)(2,1)S(1)}, bf16[1,1,2,2,192,256]{5,4,3,2,1,0:T(8,128)(2,1)S(1)}, u32[]{:S(2)}, u32[]{:S(2)}) collective-permute-start(bf16[1,1,2,2,192,256]{5,4,3,2,1,0:T(8,128)(2,1)S(1)} %get-tuple-element.85), channel_id=1, source_target_pairs={{1,0},{2,1},{3,2},{4,3},{5,4},{6,5},{7,6},{0,7},{9,8},{10,9},{11,1... | collective-permute-start | bytes 1179656 | tf_op jit(solution)/shard_map/ppermute | solution.py:23
  8.5 9.4 %collective-permute-start = (bf16[1,1,2,2,192,256]{5,4,3,2,1,0:T(8,128)(2,1)S(1)}, bf16[1,1,2,2,192,256]{5,4,3,2,1,0:T(8,128)(2,1)S(1)}, u32[]{:S(2)}, u32[]{:S(2)}) collective-permute-start(bf16[1,1,2,2,192,256]{5,4,3,2,1,0:T(8,128)(2,1)S(1)} %get-tuple-element.84), channel_id=1, source_target_pairs={{0,1},{1,2},{2,3},{3,4},{4,5},{5,6},{6,7},{7,0},{8,9},{9,10},{10,1... | collective-permute-start | bytes 1179656 | tf_op jit(solution)/shard_map/ppermute | solution.py:21
  29.8 8.3 %copy-start.7 = (f32[6,192,256]{2,1,0:T(8,128)S(1)}, f32[6,192,256]{2,1,0:T(8,128)}, u32[]{:S(2)}) copy-start(f32[6,192,256]{2,1,0:T(8,128)} %param.6) | copy-start | bytes 3538948
  38.1 3.6 %copy-start.17 = (f32[1,6,192,256]{3,2,1,0:T(8,128)S(1)}, f32[1,6,192,256]{3,2,1,0:T(8,128)}, u32[]{:S(2)}) copy-start(f32[1,6,192,256]{3,2,1,0:T(8,128)} %param.5) | copy-start | bytes 3538948
  41.7 1.4 copy-start.4
  52.3 11.0 %collective-permute-start.3 = (f32[1,1,2,2,192,256]{5,4,3,2,1,0:T(8,128)S(1)}, f32[1,1,2,2,192,256]{5,4,3,2,1,0:T(8,128)S(1)}, u32[]{:S(2)}, u32[]{:S(2)}) collective-permute-start(f32[1,1,2,2,192,256]{5,4,3,2,1,0:T(8,128)S(1)} %get-tuple-element.79), channel_id=1, source_target_pairs={{1,0},{2,1},{3,2},{4,3},{5,4},{6,5},{7,6},{0,7},{9,8},{10,9},{11,1... | collective-permute-start | bytes 2359304 | tf_op jit(solution)/shard_map/ppermute | solution.py:23
  52.3 21.7 %collective-permute-start.2 = (f32[1,1,2,2,192,256]{5,4,3,2,1,0:T(8,128)S(1)}, f32[1,1,2,2,192,256]{5,4,3,2,1,0:T(8,128)S(1)}, u32[]{:S(2)}, u32[]{:S(2)}) collective-permute-start(f32[1,1,2,2,192,256]{5,4,3,2,1,0:T(8,128)S(1)} %get-tuple-element.78), channel_id=1, source_target_pairs={{0,1},{1,2},{2,3},{3,4},{4,5},{5,6},{6,7},{7,0},{8,9},{9,10},{10,1... | collective-permute-start | bytes 2359304 | tf_op jit(solution)/shard_map/ppermute | solution.py:21
  63.3 10.7 %copy-start.23 = (f32[1,1,2,2,192,256]{5,4,3,2,1,0:T(8,128)}, f32[1,1,2,2,192,256]{5,4,3,2,1,0:T(8,128)S(1)}, u32[]{:S(2)}) copy-start(f32[1,1,2,2,192,256]{5,4,3,2,1,0:T(8,128)S(1)} %collective-permute-done.3) | copy-start | bytes 2359300
  84.0 6.2 %copy-start.28 = (f32[1,1,2]{2,1,0:T(1,128)S(1)}, f32[1,1,2]{2,1,0:T(1,128)}, u32[]{:S(2)}) copy-start(f32[1,1,2]{2,1,0:T(1,128)} %pad_maximum_fusion.6) | copy-start | bytes 28
  114.1 2.2 copy-start.2
  114.1 2.3 copy-start.5
  114.1 2.7 copy-start.18
  116.3 1.0 copy-start.9
  116.3 1.6 copy-start.11
  140.9 2.0 copy-start.3
  140.9 2.0 copy-start.6
  140.9 2.8 copy-start.10
  141.0 3.2 %copy-start.12 = (f32[1,1,1,6,192,256]{5,4,3,2,1,0:T(8,128)S(1)}, f32[1,1,1,6,192,256]{5,4,3,2,1,0:T(8,128)}, u32[]{:S(2)}) copy-start(f32[1,1,1,6,192,256]{5,4,3,2,1,0:T(8,128)} %copy-done.11) | copy-start | bytes 3538948
  141.0 3.5 %copy-start.19 = (f32[1,6,192,256]{3,2,1,0:T(8,128)S(1)}, f32[1,6,192,256]{3,2,1,0:T(8,128)}, u32[]{:S(2)}) copy-start(f32[1,6,192,256]{3,2,1,0:T(8,128)} %param.5) | copy-start | bytes 3538948
  151.9 21.5 %collective-permute-start.5 = (f32[1,1,2,2,192,256]{5,4,3,2,1,0:T(8,128)S(1)}, f32[1,1,2,2,192,256]{5,4,3,2,1,0:T(8,128)S(1)}, u32[]{:S(2)}, u32[]{:S(2)}) collective-permute-start(f32[1,1,2,2,192,256]{5,4,3,2,1,0:T(8,128)S(1)} %get-tuple-element.55), channel_id=1, source_target_pairs={{1,0},{2,1},{3,2},{4,3},{5,4},{6,5},{7,6},{0,7},{9,8},{10,9},{11,1... | collective-permute-start | bytes 2359304 | tf_op jit(solution)/shard_map/ppermute | solution.py:23
  155.4 18.9 %collective-permute-start.4 = (f32[1,1,2,2,192,256]{5,4,3,2,1,0:T(8,128)S(1)}, f32[1,1,2,2,192,256]{5,4,3,2,1,0:T(8,128)S(1)}, u32[]{:S(2)}, u32[]{:S(2)}) collective-permute-start(f32[1,1,2,2,192,256]{5,4,3,2,1,0:T(8,128)S(1)} %get-tuple-element.54), channel_id=1, source_target_pairs={{0,1},{1,2},{2,3},{3,4},{4,5},{5,6},{6,7},{7,0},{8,9},{9,10},{10,1... | collective-permute-start | bytes 2359304 | tf_op jit(solution)/shard_map/ppermute | solution.py:21
  175.3 9.9 %copy-start.8 = (f32[6,192,256]{2,1,0:T(8,128)S(1)}, f32[6,192,256]{2,1,0:T(8,128)}, u32[]{:S(2)}) copy-start(f32[6,192,256]{2,1,0:T(8,128)} %param.6) | copy-start | bytes 3538948
  188.7 3.2 %copy-start.27 = (f32[1,2]{1,0:T(1,128)S(1)}, f32[1,2]{1,0:T(1,128)}, u32[]{:S(2)}) copy-start(f32[1,2]{1,0:T(1,128)} %param.9) | copy-start | bytes 28
  212.8 1.3 copy-start.21
  212.8 2.5 copy-start.22
  213.1 2.6 copy-start.13
  213.1 2.6 copy-start.15
  219.1 1.3 copy-start.14
  219.1 1.6 copy-start.16
  220.8 2.1 copy-start.20
  (4 other events, 3.8 us)
Sparse Core Ops, SparseCore 0:
  219.3 59.3 reduce-scatter.1
where the time goes:
time: 310 us; the launch traced here: 309 us
  blocking collectives  84 us (27%)
  other arithmetic  60.8 us (20%)
  local copies, waits for them, and re-layouts  53.7 us (17%)
  between operations  46.6 us (15%)
  matrix products  29.6 us (10%)
  waiting for transfers between devices  29.5 us (10%)
  starting transfers between devices  4.66 us (2%)
    psum x1, blocking collectives, per_device(): trace_estimate = lax.psum(local_trace, ('node', 'grid'))  44 us
    dot_general x1, matrix products, per_device(): jnp.einsum('pzxy,spczxy->sc', probes, solution, precision=highest) / PROBES  29.6 us
    psum x2, blocking collectives, residual_norms(): return lax.psum(bilinear(vector, vector), 'grid')  27.8 us
    add x3, other arithmetic, hamiltonian_apply(): near_weight * near_sum + far_weight * far_sum + self_weight * middle  27.3 us
    ppermute x3, waiting for transfers between devices, with_halo(): lax.ppermute(head, axis, [((i + 1) % count, i) for i in range(count)])  15.5 us
    slice x6, local copies, waits for them, and re-layouts, hamiltonian_apply(): jnp.roll(middle, -2, 5)  14.3 us
    ppermute x3, waiting for transfers between devices, with_halo(): lax.ppermute(tail, axis, [(i, (i + 1) % count) for i in range(count)])  14 us
    slice x6, local copies, waits for them, and re-layouts, hamiltonian_apply(): jnp.roll(middle, -1, 5)  12.4 us
  transfers between devices with their start and end apart: 7, of which 5 were waited for; matrix products, arithmetic and copies ran while one was open for 16% of the time, Pallas kernels for 0%

commit v1 on v0

--- a/solution.py
+++ b/solution.py
@@ -2,6 +2,7 @@
 import jax.numpy as jnp
 from jax import lax
 from jax.sharding import PartitionSpec as P
+from jax.lax import psum
 
 PROBES = 1
 ITERS = 2
@@ -191,7 +192,12 @@
     moments = lax.psum_scatter(moment_terms, "node", scatter_dimension=4, tiled=True)
     inner_sums = jnp.einsum("pzxy,spczxy->sc", probes, solution, precision=highest) / PROBES
     local_trace = jnp.sum(complex_times(quad_weights, inner_sums), axis=0)
-    trace_estimate = lax.psum(local_trace, ("node", "grid"))
+
+    def register_sheet(array_in, axis_tag, ax_name):
+        long_array = psum(psum(array_in, axis_tag), ax_name)
+        return long_array
+
+    trace_estimate = register_sheet(local_trace, "grid", "node")
     return (moments, trace_estimate)
 
 

time: 310 us -> 294 us (0.948)
  the two profiles are of different devices: /device:TPU:12 before, /device:TPU:0 now
where the time goes in v1:
time: 294 us; the launch traced here: 293 us
  blocking collectives  70 us (24%)
  other arithmetic  60.5 us (21%)
  local copies, waits for them, and re-layouts  53.6 us (18%)
  between operations  46.3 us (16%)
  matrix products  29.6 us (10%)
  waiting for transfers between devices  27.4 us (9%)
  starting transfers between devices  5.97 us (2%)
    dot_general x1, matrix products, per_device(): jnp.einsum('pzxy,spczxy->sc', probes, solution, precision=highest) / PROBES  29.6 us
    psum x2, blocking collectives, residual_norms(): return lax.psum(bilinear(vector, vector), 'grid')  29.2 us
    add x3, other arithmetic, hamiltonian_apply(): near_weight * near_sum + far_weight * far_sum + self_weight * middle  27.3 us
    psum x2, blocking collectives, register_sheet(): long_array = psum(psum(array_in, axis_tag), ax_name)  24 us
    ppermute x3, waiting for transfers between devices, with_halo(): lax.ppermute(head, axis, [((i + 1) % count, i) for i in range(count)])  21.5 us
    psum x1, blocking collectives, per_device(): curvature = lax.psum(bilinear(center_part, center(applied, extent)), 'grid')  16.9 us
    slice x6, local copies, waits for them, and re-layouts, hamiltonian_apply(): jnp.roll(middle, -2, 5)  14.2 us
    slice x6, local copies, waits for them, and re-layouts, hamiltonian_apply(): jnp.roll(middle, -1, 5)  12.5 us
  transfers between devices with their start and end apart: 7, of which 6 were waited for; matrix products, arithmetic and copies ran while one was open for 16% of the time, Pallas kernels for 0%

profile of v1, /device:TPU:0, one launch (start us, length us, event | category | flops | bytes accessed | tf_op | source)
XLA Modules:
  0.0 293.3 jit_solution(15378256440048642435)
XLA Ops:
  8.5 4.5 %collective-permute-start.1 = (bf16[1,1,2,2,192,256]{5,4,3,2,1,0:T(8,128)(2,1)S(1)}, bf16[1,1,2,2,192,256]{5,4,3,2,1,0:T(8,128)(2,1)S(1)}, u32[]{:S(2)}, u32[]{:S(2)}) collective-permute-start(bf16[1,1,2,2,192,256]{5,4,3,2,1,0:T(8,128)(2,1)S(1)} %get-tuple-element.85), channel_id=1, source_target_pairs={{1,0},{2,1},{3,2},{4,3},{5,4},{6,5},{7,6},{0,7},{9,8},{10,9},{11,1... | collective-permute-start | bytes 1179656 | tf_op jit(solution)/shard_map/ppermute | solution.py:24
  20.6 2.9 %collective-permute-done = bf16[1,1,2,2,192,256]{5,4,3,2,1,0:T(8,128)(2,1)S(1)} collective-permute-done((bf16[1,1,2,2,192,256]{5,4,3,2,1,0:T(8,128)(2,1)S(1)}, bf16[1,1,2,2,192,256]{5,4,3,2,1,0:T(8,128)(2,1)S(1)}, u32[]{:S(2)}, u32[]{:S(2)}) %collective-permute-start) | collective-permute-done | bytes 393248 | tf_op jit(solution)/shard_map/ppermute | solution.py:22
  24.4 2.2 fusion.79
  28.0 2.6 fusion.78
  30.6 2.9 fusion.76
  35.4 8.3 %fusion.24 = f32[1,1,2,6,192,256]{5,4,3,2,1,0:T(8,128)} fusion(f32[1,1,2,10,192,256]{5,4,3,2,1,0:T(8,128)S(1)} %maximum_convert_fusion, f32[1,1,2,6,191,256]{5,4,3,2,1,0:T(8,128)S(1)} %get-tuple-element.31, f32[1,1,2,6,1,256]{5,4,3,2,1,0:T(1,128)S(1)} %get-tuple-element.83, f32[1,1,2,6,1,256]{5,4,3,2,1,0:T(1,128)S(1)} %get-tuple-element.82, ...), kind=kLoop, calls=%fused_computation.38 | loop fusion | flops 13565952 | bytes 33030144 | tf_op jit(solution)/shard_map/add | solution.py:45
  43.7 3.5 %fusion.54 = (f32[1,1,1,6,192,256]{5,4,3,2,1,0:T(8,128)S(1)}, f32[1,1,1,6,192,256]{5,4,3,2,1,0:T(8,128)S(1)}) fusion(f32[1,1,2,6,192,256]{5,4,3,2,1,0:T(8,128)} %fusion.24, f32[6,192,256]{2,1,0:T(8,128)S(1)} %copy-done.7, f32[1,1,2,10,192,256]{5,4,3,2,1,0:T(8,128)S(1)} %maximum_convert_fusion, f32[]{:T(128)} %bitcast.6, f32[]{:T(128)} %bitcast.4), kind=kLoop, calls=%fused_computation.97 | loop fusion | flops 4128768 | bytes 8257544 | tf_op jit(solution)/shard_map/stack | solution.py:62
  50.5 3.0 %fusion.95 = (f32[1,1,2,6,192,255]{5,4,3,2,1,0:T(8,128)}, f32[1,1,2,6,192,255]{5,4,3,2,1,0:T(8,128)}) fusion(f32[1,1,2,6,192,256]{5,4,3,2,1,0:T(8,128)S(1)} %maximum_subtract_fusion), kind=kLoop, calls=%fused_computation.178 | loop fusion | bytes 9400320 | tf_op jit(solution)/shard_map/jit(_roll_static)/slice | solution.py:37
  58.6 1.9 pad_maximum_fusion.6
  60.5 2.6 fusion.93
  63.1 2.9 fusion.91
  66.0 9.4 %collective-permute-done.3 = f32[1,1,2,2,192,256]{5,4,3,2,1,0:T(8,128)S(1)} collective-permute-done((f32[1,1,2,2,192,256]{5,4,3,2,1,0:T(8,128)S(1)}, f32[1,1,2,2,192,256]{5,4,3,2,1,0:T(8,128)S(1)}, u32[]{:S(2)}, u32[]{:S(2)}) %collective-permute-start.3) | collective-permute-done | bytes 786464 | tf_op jit(solution)/shard_map/ppermute | solution.py:24
  75.5 2.1 collective-permute-done.2
  78.5 9.1 %fusion.14 = f32[1,1,2,6,192,256]{5,4,3,2,1,0:T(8,128)S(1)} fusion(f32[1,1,2,6,192,256]{5,4,3,2,1,0:T(8,128)S(1)} %maximum_subtract_fusion, f32[1,1,2,2,192,256]{5,4,3,2,1,0:T(8,128)} %copy-done.23, f32[1,1,2,2,192,256]{5,4,3,2,1,0:T(8,128)} %copy-done.24, f32[1,1,2,6,191,256]{5,4,3,2,1,0:T(8,128)} %get-tuple-element.75, ...), kind=kLoop, calls=%fused_computation.23 | loop fusion | flops 15925248 | bytes 25165824 | tf_op jit(solution)/shard_map/add | solution.py:45
  87.6 4.1 %fusion.64 = (f32[]{:T(128)}, f32[]{:T(128)}, f32[6,192,256]{2,1,0:T(8,128)}, f32[6,192,256]{2,1,0:T(8,128)}) fusion(f32[1,1,2,6,192,256]{5,4,3,2,1,0:T(8,128)S(1)} %maximum_subtract_fusion, f32[6,192,256]{2,1,0:T(8,128)S(1)} %copy-done.7, f32[1,1,2,6,192,256]{5,4,3,2,1,0:T(8,128)S(1)} %fusion.14, f32[]{:T(128)} %bitcast.6, f32[]{:T(128)} %bitcast.4), kind=kLoop, calls=%fused_computation.124 | loop fusion | flops 6488062 | bytes 8257552 | tf_op jit(solution)/shard_map/reduce_sum | solution.py:66
  91.8 2.0 pad_maximum_fusion.7
  93.9 15.6 %all-reduce.1 = (f32[1,1,2]{2,1,0:T(1,128)S(1)}, f32[1,1,2]{2,1,0:T(1,128)S(1)}) all-reduce(f32[1,1,2]{2,1,0:T(1,128)S(1)} %copy-done.28, f32[1,1,2]{2,1,0:T(1,128)} %pad_maximum_fusion.7), channel_id=1, replica_groups=mesh['node'=4,'grid'=8] {'grid'}, use_global_device_ids=true, to_apply=%region_2.3 | all-reduce | flops 4 | bytes 32 | tf_op jit(solution)/shard_map/psum | solution.py:124
  118.9 2.1 subtract_bitcast_fusion.1
  126.1 13.6 %psum.44 = f32[1,1,2]{2,1,0:T(1,128)S(1)} all-reduce(f32[1,1,2]{2,1,0:T(1,128)S(1)} %pad_maximum_fusion.8), channel_id=1, replica_groups=mesh['node'=4,'grid'=8] {'grid'}, use_global_device_ids=true, to_apply=%region_8.9 | all-reduce | flops 2 | bytes 16 | tf_op jit(solution)/shard_map/psum | solution.py:124
  145.5 1.9 multiply_subtract_fusion.1
  150.2 3.0 %fusion.86 = (f32[1,1,2,6,192,255]{5,4,3,2,1,0:T(8,128)}, f32[1,1,2,6,192,255]{5,4,3,2,1,0:T(8,128)}) fusion(f32[1,1,2,6,192,256]{5,4,3,2,1,0:T(8,128)S(1)} %maximum_add_fusion.9), kind=kLoop, calls=%fused_computation.169 | loop fusion | bytes 9400320 | tf_op jit(solution)/shard_map/jit(_roll_static)/slice | solution.py:37
  156.9 2.6 fusion.84
  159.6 2.9 fusion.82
  162.5 11.0 %collective-permute-done.5 = f32[1,1,2,2,192,256]{5,4,3,2,1,0:T(8,128)S(1)} collective-permute-done((f32[1,1,2,2,192,256]{5,4,3,2,1,0:T(8,128)S(1)}, f32[1,1,2,2,192,256]{5,4,3,2,1,0:T(8,128)S(1)}, u32[]{:S(2)}, u32[]{:S(2)}) %collective-permute-start.5) | collective-permute-done | bytes 786464 | tf_op jit(solution)/shard_map/ppermute | solution.py:24
  175.2 9.9 %fusion.6 = f32[1,1,2,6,192,256]{5,4,3,2,1,0:T(8,128)} fusion(f32[1,1,2,6,192,256]{5,4,3,2,1,0:T(8,128)S(1)} %maximum_add_fusion.9, f32[1,1,2,2,192,256]{5,4,3,2,1,0:T(8,128)} %copy-done.25, f32[1,1,2,2,192,256]{5,4,3,2,1,0:T(8,128)} %copy-done.26, f32[1,1,2,6,191,256]{5,4,3,2,1,0:T(8,128)S(1)} %get-tuple-element.51, ...), kind=kLoop, calls=%fused_computation.15 | loop fusion | flops 15925248 | bytes 25165824 | tf_op jit(solution)/shard_map/add | solution.py:45
  185.1 3.4 %fusion.40 = (f32[6,192,256]{2,1,0:T(8,128)S(1)}, f32[6,192,256]{2,1,0:T(8,128)S(1)}) fusion(f32[1,1,2,6,192,256]{5,4,3,2,1,0:T(8,128)} %fusion.6, f32[6,192,256]{2,1,0:T(8,128)S(1)} %copy-done.8, f32[1,1,2,6,192,256]{5,4,3,2,1,0:T(8,128)S(1)} %maximum_add_fusion.9, f32[]{:T(128)} %bitcast.6, f32[]{:T(128)} %bitcast.4), kind=kLoop, calls=%fused_computation.79 | loop fusion | flops 4128768 | bytes 8257544 | tf_op jit(solution)/shard_map/sub | solution.py:51
  191.8 16.9 %psum.45 = f32[1,1,2]{2,1,0:T(1,128)S(1)} all-reduce(f32[1,1,2]{2,1,0:T(1,128)} %pad_maximum_fusion.9), channel_id=1, replica_groups=mesh['node'=4,'grid'=8] {'grid'}, use_global_device_ids=true, to_apply=%region_11.12 | all-reduce | flops 2 | bytes 16 | tf_op jit(solution)/shard_map/psum | solution.py:162
  220.7 2.6 pad_maximum_fusion
  225.0 2.1 fusion.108
  227.1 29.6 %fusion.68 = f32[1,2]{1,0:T(1,128)S(1)} fusion(f32[6,192,256,1]{2,1,0,3:T(8,128)S(1)} %bitcast.197, f32[2,6,192,256]{3,2,1,0:T(8,128)S(1)} %fusion.108), kind=kOutput, calls=%fused_computation.145 | convolution fusion | flops 7077888 | bytes 3538952 | tf_op jit(solution)/shard_map/pzxy,spczxy->sc/dot_general | solution.py:193
  262.5 13.6 %psum.46 = f32[2]{0:T(128)S(1)} all-reduce(f32[2]{0:T(128)S(1)} %maximum_bitcast_fusion.1), channel_id=1, replica_groups=mesh['node'=4,'grid'=8] {'grid'}, use_global_device_ids=true, to_apply=%region_13.14 | all-reduce | flops 2 | bytes 16 | tf_op jit(solution)/shard_map/psum | solution.py:197
  276.1 10.4 %psum.47 = f32[2]{0:T(128)} all-reduce(f32[2]{0:T(128)S(1)} %psum.46), channel_id=1, replica_groups=mesh['node'=4,'grid'=8] {'node'}, use_global_device_ids=true, to_apply=%region_14.15 | all-reduce | flops 2 | bytes 16 | tf_op jit(solution)/shard_map/psum | solution.py:197
  (108 shorter events, 41.6 us)
Async XLA Ops:
  7.2 16.4 %copy-start = (bf16[1,1,2,6,192,256]{5,4,3,2,1,0:T(8,128)(2,1)S(1)}, bf16[1,1,2,6,192,256]{5,4,3,2,1,0:T(8,128)(2,1)}, u32[]{:S(2)}) copy-start(bf16[1,1,2,6,192,256]{5,4,3,2,1,0:T(8,128)(2,1)} %param.7) | copy-start | bytes 3538948
  7.2 279.3 %reduce-scatter.2.cloned.1.call-start = ((), (), s32[]{:S(2)}) async-start(), calls=%async_computation.1 | async-start | bytes 5898240 | tf_op jit(solution)/shard_map/reduce_scatter | solution.py:192
  8.5 12.1 %collective-permute-start.1 = (bf16[1,1,2,2,192,256]{5,4,3,2,1,0:T(8,128)(2,1)S(1)}, bf16[1,1,2,2,192,256]{5,4,3,2,1,0:T(8,128)(2,1)S(1)}, u32[]{:S(2)}, u32[]{:S(2)}) collective-permute-start(bf16[1,1,2,2,192,256]{5,4,3,2,1,0:T(8,128)(2,1)S(1)} %get-tuple-element.85), channel_id=1, source_target_pairs={{1,0},{2,1},{3,2},{4,3},{5,4},{6,5},{7,6},{0,7},{9,8},{10,9},{11,1... | collective-permute-start | bytes 1179656 | tf_op jit(solution)/shard_map/ppermute | solution.py:24
  13.0 10.5 %collective-permute-start = (bf16[1,1,2,2,192,256]{5,4,3,2,1,0:T(8,128)(2,1)S(1)}, bf16[1,1,2,2,192,256]{5,4,3,2,1,0:T(8,128)(2,1)S(1)}, u32[]{:S(2)}, u32[]{:S(2)}) collective-permute-start(bf16[1,1,2,2,192,256]{5,4,3,2,1,0:T(8,128)(2,1)S(1)} %get-tuple-element.84), channel_id=1, source_target_pairs={{0,1},{1,2},{2,3},{3,4},{4,5},{5,6},{6,7},{7,0},{8,9},{9,10},{10,1... | collective-permute-start | bytes 1179656 | tf_op jit(solution)/shard_map/ppermute | solution.py:22
  35.4 8.3 %copy-start.7 = (f32[6,192,256]{2,1,0:T(8,128)S(1)}, f32[6,192,256]{2,1,0:T(8,128)}, u32[]{:S(2)}) copy-start(f32[6,192,256]{2,1,0:T(8,128)} %param.6) | copy-start | bytes 3538948
  43.6 3.5 %copy-start.17 = (f32[1,6,192,256]{3,2,1,0:T(8,128)S(1)}, f32[1,6,192,256]{3,2,1,0:T(8,128)}, u32[]{:S(2)}) copy-start(f32[1,6,192,256]{3,2,1,0:T(8,128)} %param.5) | copy-start | bytes 3538948
  47.1 1.4 copy-start.4
  57.7 17.8 %collective-permute-start.3 = (f32[1,1,2,2,192,256]{5,4,3,2,1,0:T(8,128)S(1)}, f32[1,1,2,2,192,256]{5,4,3,2,1,0:T(8,128)S(1)}, u32[]{:S(2)}, u32[]{:S(2)}) collective-permute-start(f32[1,1,2,2,192,256]{5,4,3,2,1,0:T(8,128)S(1)} %get-tuple-element.79), channel_id=1, source_target_pairs={{1,0},{2,1},{3,2},{4,3},{5,4},{6,5},{7,6},{0,7},{9,8},{10,9},{11,1... | collective-permute-start | bytes 2359304 | tf_op jit(solution)/shard_map/ppermute | solution.py:24
  58.6 19.0 %collective-permute-start.2 = (f32[1,1,2,2,192,256]{5,4,3,2,1,0:T(8,128)S(1)}, f32[1,1,2,2,192,256]{5,4,3,2,1,0:T(8,128)S(1)}, u32[]{:S(2)}, u32[]{:S(2)}) collective-permute-start(f32[1,1,2,2,192,256]{5,4,3,2,1,0:T(8,128)S(1)} %get-tuple-element.78), channel_id=1, source_target_pairs={{0,1},{1,2},{2,3},{3,4},{4,5},{5,6},{6,7},{7,0},{8,9},{9,10},{10,1... | collective-permute-start | bytes 2359304 | tf_op jit(solution)/shard_map/ppermute | solution.py:22
  75.5 2.1 copy-start.23
  87.6 6.2 %copy-start.28 = (f32[1,1,2]{2,1,0:T(1,128)S(1)}, f32[1,1,2]{2,1,0:T(1,128)}, u32[]{:S(2)}) copy-start(f32[1,1,2]{2,1,0:T(1,128)} %pad_maximum_fusion.6) | copy-start | bytes 28
  118.9 2.2 copy-start.2
  118.9 2.3 copy-start.5
  118.9 2.7 copy-start.18
  121.0 1.0 copy-start.9
  121.0 1.6 copy-start.11
  145.5 2.0 copy-start.3
  145.5 2.0 copy-start.6
  145.5 2.8 copy-start.10
  145.5 3.2 %copy-start.12 = (f32[1,1,1,6,192,256]{5,4,3,2,1,0:T(8,128)S(1)}, f32[1,1,1,6,192,256]{5,4,3,2,1,0:T(8,128)}, u32[]{:S(2)}) copy-start(f32[1,1,1,6,192,256]{5,4,3,2,1,0:T(8,128)} %copy-done.11) | copy-start | bytes 3538948
  145.5 3.5 %copy-start.19 = (f32[1,6,192,256]{3,2,1,0:T(8,128)S(1)}, f32[1,6,192,256]{3,2,1,0:T(8,128)}, u32[]{:S(2)}) copy-start(f32[1,6,192,256]{3,2,1,0:T(8,128)} %param.5) | copy-start | bytes 3538948
  156.4 17.0 %collective-permute-start.5 = (f32[1,1,2,2,192,256]{5,4,3,2,1,0:T(8,128)S(1)}, f32[1,1,2,2,192,256]{5,4,3,2,1,0:T(8,128)S(1)}, u32[]{:S(2)}, u32[]{:S(2)}) collective-permute-start(f32[1,1,2,2,192,256]{5,4,3,2,1,0:T(8,128)S(1)} %get-tuple-element.55), channel_id=1, source_target_pairs={{1,0},{2,1},{3,2},{4,3},{5,4},{6,5},{7,6},{0,7},{9,8},{10,9},{11,1... | collective-permute-start | bytes 2359304 | tf_op jit(solution)/shard_map/ppermute | solution.py:24
  156.4 17.8 %collective-permute-start.4 = (f32[1,1,2,2,192,256]{5,4,3,2,1,0:T(8,128)S(1)}, f32[1,1,2,2,192,256]{5,4,3,2,1,0:T(8,128)S(1)}, u32[]{:S(2)}, u32[]{:S(2)}) collective-permute-start(f32[1,1,2,2,192,256]{5,4,3,2,1,0:T(8,128)S(1)} %get-tuple-element.54), channel_id=1, source_target_pairs={{0,1},{1,2},{2,3},{3,4},{4,5},{5,6},{6,7},{7,0},{8,9},{9,10},{10,1... | collective-permute-start | bytes 2359304 | tf_op jit(solution)/shard_map/ppermute | solution.py:22
  175.1 9.9 %copy-start.8 = (f32[6,192,256]{2,1,0:T(8,128)S(1)}, f32[6,192,256]{2,1,0:T(8,128)}, u32[]{:S(2)}) copy-start(f32[6,192,256]{2,1,0:T(8,128)} %param.6) | copy-start | bytes 3538948
  188.5 3.1 %copy-start.27 = (f32[1,2]{1,0:T(1,128)S(1)}, f32[1,2]{1,0:T(1,128)}, u32[]{:S(2)}) copy-start(f32[1,2]{1,0:T(1,128)} %param.9) | copy-start | bytes 28
  217.0 1.3 copy-start.21
  217.0 2.5 copy-start.22
  217.3 2.6 copy-start.13
  217.3 2.6 copy-start.15
  223.3 1.3 copy-start.14
  223.3 1.6 copy-start.16
  225.0 2.1 copy-start.20
  (4 other events, 3.7 us)
Sparse Core Ops, SparseCore 0:
  223.5 55.2 reduce-scatter.1
